TPU v7x, 128 devices: a whole 4x4x4 slice. The times are simulated.
128 devices in a mesh: ctx: 16 (over y_lo, z, core), head: 8 (over x, y_hi).
Axes of the slice: x: 4, y: 4 (y_hi: 2, y_lo: 2; y = y_hi * 2 + y_lo), z: 4, core: 2. Of those that a mesh axis runs over, the one named last changes fastest.
Arguments:
- queries: bfloat16 [2048, 36864], P('ctx', 'head'), may hold values from -296 to 296
- latent_keys: bfloat16 [2048, 576], P('ctx'), may hold values from -9 to 9
- block_order: int32 [16], replicated, may hold values from 0 to 15, each once
- out_grad: bfloat16 [2048, 32768], P('ctx', 'head'), may hold values from -6 to 6
Outputs:
- attended: bfloat16 [2048, 32768], P('ctx', 'head')
- query_grad: bfloat16 [2048, 36864], P('ctx', 'head')
- latent_grad: bfloat16 [2048, 576], P('ctx')
Inputs may be any that keep to these rules, and one draw needn't show every extreme that they name: `block_order`: a permutation: each block index once.
All inputs are finite; a program needn't handle non-finite values.
Results may differ from a plain program's by a relative error of at most 0.034.
Values may be sent and summed in bfloat16 or wider, within the bound.
A program may use at most 64 MiB of HBM per device.

v0:
```python
import jax
import jax.numpy as jnp
from jax import lax
from jax.sharding import PartitionSpec as P

LATENT = 512
ROPE = 64
score_scale = 192.0 ** (-0.5)
masked_value = -1e30


def row_positions(block_order, first_row, count, shard_rows):
    rows = first_row + jnp.arange(count, dtype=jnp.int32)
    owner = rows // shard_rows
    blocks = block_order.shape[0]
    onehot = (owner[:, None] == jnp.arange(blocks, dtype=jnp.int32)[None, :]).astype(jnp.int32)
    base = jnp.sum(onehot * block_order[None, :], axis=1)
    return base * shard_rows + rows % shard_rows


def local(queries, latent_keys, block_order, out_grad):
    kdim = LATENT + ROPE
    shard_rows = latent_keys.shape[0]
    head_count = queries.shape[1] // kdim
    query_three = queries.reshape(shard_rows, head_count, kdim)
    grad_three = out_grad.reshape(shard_rows, head_count, LATENT)
    own_index = lax.axis_index("ctx")
    query_pos = row_positions(block_order, own_index * shard_rows, shard_rows, shard_rows)

    def piece_scores(piece, start):
        score = (
            jnp.einsum("thd,pd->htp", query_three, piece, preferred_element_type=jnp.float32)
            * score_scale
        )
        key_pos = row_positions(block_order, start, piece.shape[0], shard_rows)
        visible = key_pos[None, :] <= query_pos[:, None]
        return (jnp.where(visible[None], score, masked_value), visible)

    running_max = jnp.full((head_count, shard_rows), masked_value, jnp.float32)
    score, visible = piece_scores(
        lax.all_gather(latent_keys, "ctx", axis=0, tiled=True), jnp.int32(0)
    )
    new_max = jnp.maximum(running_max, jnp.max(score, axis=2))
    weights = jnp.where(visible[None], jnp.exp(score - new_max[:, :, None]), 0.0)
    new_sum = jnp.sum(weights, axis=2)
    lse = new_max + jnp.log(new_sum)
    piece = lax.all_gather(latent_keys, "ctx", axis=0, tiled=True)
    score, visible = piece_scores(piece, jnp.int32(0))
    prob_b = jnp.where(visible[None], jnp.exp(score - lse[:, :, None]), 0.0).astype(jnp.bfloat16)
    accum = jnp.einsum("htp,pe->the", prob_b, piece[:, :LATENT], preferred_element_type=jnp.float32)
    attended = accum.astype(jnp.bfloat16)
    delta = jnp.sum(attended.astype(jnp.float32) * grad_three.astype(jnp.float32), axis=2).T
    piece = lax.all_gather(latent_keys, "ctx", axis=0, tiled=True)
    score, visible = piece_scores(piece, jnp.int32(0))
    prob = jnp.where(visible[None], jnp.exp(score - lse[:, :, None]), 0.0)
    prob_b = prob.astype(jnp.bfloat16)
    dprob = jnp.einsum(
        "the,pe->htp", grad_three, piece[:, :LATENT], preferred_element_type=jnp.float32
    )
    dscore = (prob * (dprob - delta[:, :, None])).astype(jnp.bfloat16)
    query_accum = jnp.einsum("htp,pd->thd", dscore, piece, preferred_element_type=jnp.float32)
    key_part = score_scale * jnp.einsum(
        "htp,thd->pd", dscore, query_three, preferred_element_type=jnp.float32
    )
    value_part = jnp.einsum("htp,the->pe", prob_b, grad_three, preferred_element_type=jnp.float32)
    term = key_part + jnp.pad(value_part, ((0, 0), (0, ROPE)))
    key_accum = term
    query_accum, key_accum = (query_accum, key_accum)
    query_grad = (
        (score_scale * query_accum).astype(jnp.bfloat16).reshape(shard_rows, head_count * kdim)
    )
    partial_rows = lax.psum_scatter(key_accum, "ctx", scatter_dimension=0, tiled=True)
    latent_grad = lax.psum(partial_rows, "head").astype(jnp.bfloat16)
    return (attended.reshape(shard_rows, head_count * LATENT), query_grad, latent_grad)


def solution(mesh):
    placed = (P("ctx", "head"), P("ctx", None), P(), P("ctx", "head"))
    return jax.shard_map(
        local,
        mesh=mesh,
        in_specs=placed,
        out_specs=(P("ctx", "head"), P("ctx", "head"), P("ctx", None)),
        check_vma=False,
    )
```

profile of v0, /device:TPU:0, one launch (start us, length us, event | category | flops | bytes accessed | tf_op | source)
XLA Modules:
  0.0 196.5 jit_solution(11976603212448171671)
XLA Ops:
  7.2 0.0 copy-start
  7.2 0.0 copy-start.3
  7.2 0.0 all-gather.2.cloned.1.call-start
  7.2 0.7 all-gather.2.cloned.1.call-update
  7.9 0.0 reduce-scatter.2.cloned.1.call-start
  8.0 1.6 copy.34
  9.6 1.3 copy.37
  10.9 0.0 copy-done
  10.9 0.7 copy.30
  11.7 0.0 copy-done.3
  11.7 0.1 select_reduce_fusion.2
  11.8 0.1 select_reduce_fusion.1
  11.9 0.3 broadcast_compare_fusion
  12.2 38.2 %all-gather.2.cloned.1.call-done = bf16[2048,576]{0,1:T(8,128)(2,1)} async-done(((bf16[128,576]{0,1:T(8,128)(2,1)}), bf16[2048,576]{0,1:T(8,128)(2,1)}) %all-gather.2.cloned.1.call-update) | async-done | bytes 2359312 | tf_op jit(solution)/shard_map/all_gather | solution.py:47
  50.5 5.6 %fusion.3 = (f32[8,128]{1,0:T(8,128)S(1)}, f32[2048,128,8]{1,0,2:T(8,128)S(1)}) fusion(pred[128,2048]{0,1:T(8,128)(4,1)S(1)} %broadcast_compare_fusion, bf16[128,8,576]{0,2,1:T(8,128)(2,1)S(1)} %bitcast.65, bf16[2048,576]{0,1:T(8,128)(2,1)} %all-gather.2.cloned.1.call-done), kind=kOutput, calls=%fused_computation.7 | convolution fusion | flops 2422209536 | bytes 12193792 | tf_op jit(solution)/shard_map/thd,pd->htp/dot_general | solution.py:32
  56.1 2.0 %select_reduce_fusion = f32[8,128]{1,0:T(8,128)S(1)} fusion(f32[2048,128,8]{1,0,2:T(8,128)S(1)} %get-tuple-element.13, f32[8,128]{1,0:T(8,128)S(1)} %broadcast_maximum_fusion, pred[128,2048]{0,1:T(8,128)(4,1)S(1)} %broadcast_compare_fusion), kind=kLoop, calls=%fused_computation.5 | loop fusion | flops 10484736 | bytes 8658944 | tf_op jit(solution)/shard_map/reduce_sum | solution.py:45
  58.1 0.0 copy-start.1
  58.2 0.0 copy-start.4
  58.2 2.7 %convolution_bitcast_fusion = f32[2048,512]{0,1:T(8,128)S(1)} fusion(bf16[128,8,512]{0,2,1:T(8,128)(2,1)S(1)} %bitcast.62, f32[2048,128,8]{1,0,2:T(8,128)S(1)} %get-tuple-element.13, f32[8,128]{1,0:T(8,128)S(1)} %log_add_fusion, pred[128,2048]{0,1:T(8,128)(4,1)S(1)} %broadcast_compare_fusion), kind=kOutput, calls=%fused_computation.10 | convolution fusion | flops 2157969408 | bytes 13897728 | tf_op jit(solution)/shard_map/htp,the->pe/dot_general | solution.py:65
  60.9 0.0 copy-done.1
  60.9 3.7 %multiply_reduce_fusion = (f32[128,8]{0,1:T(8,128)S(1)}, bf16[128,8,512]{2,0,1:T(8,128)(2,1)}) fusion(bf16[128,8,512]{2,0,1:T(8,128)(2,1)S(1)} %copy-done.1, bf16[2048,576]{0,1:T(8,128)(2,1)S(1)} %copy-done.4, f32[2048,128,8]{1,0,2:T(8,128)S(1)} %get-tuple-element.13, f32[8,128]{1,0:T(8,128)S(1)} %log_add_fusion, ...), kind=kOutput, calls=%fused_computation.17 | convolution fusion | flops 2160589824 | bytes 12853248 | tf_op jit(solution)/shard_map/htp,pe->the/dot_general | solution.py:50
  64.6 4.5 %fusion.1 = bf16[8,128,2048]{1,2,0:T(8,128)(2,1)S(1)} fusion(f32[2048,128,8]{1,0,2:T(8,128)S(1)} %get-tuple-element.13, bf16[128,8,512]{0,2,1:T(8,128)(2,1)S(1)} %bitcast.63, f32[8,128]{1,0:T(8,128)S(1)} %bitcast.68, f32[8,128]{1,0:T(8,128)S(1)} %log_add_fusion, pred[128,2048]{0,1:T(8,128)(4,1)S(1)} %broadcast_compare_fusion, bf16[2048,576]{0,1:T(8,128)(2,1)S(1)} %copy-done.4), kind=kOutput, calls=%fused_computation.2 | convolution fusion | flops 2162163712 | bytes 15998976 | tf_op jit(solution)/shard_map/the,pe->htp/dot_general | solution.py:57
  69.0 2.0 %copy-done.5 = bf16[8,128,2048]{1,2,0:T(8,128)(2,1)} copy-done((bf16[8,128,2048]{1,2,0:T(8,128)(2,1)}, bf16[8,128,2048]{1,2,0:T(8,128)(2,1)S(1)}, u32[]{:S(2)}) %copy-start.5) | copy-done | bytes 4194328
  71.0 4.3 %fusion.4 = f32[2048,576]{0,1:T(8,128)} fusion(f32[2048,512]{0,1:T(8,128)S(1)} %convolution_bitcast_fusion, bf16[8,128,2048]{1,2,0:T(8,128)(2,1)S(1)} %fusion.1, bf16[128,8,576]{0,2,1:T(8,128)(2,1)S(1)} %bitcast.66), kind=kOutput, calls=%fused_computation.9 | convolution fusion | flops 2418278400 | bytes 14286848 | tf_op jit(solution)/shard_map/htp,thd->pd/dot_general | solution.py:62
  75.4 0.0 reduce-scatter.2.cloned.1.call-update
  75.4 1.2 copy-done.2
  76.6 0.7 copy.33
  77.2 1.3 copy.41
  78.6 5.5 %multiply_convert_fusion = bf16[8,128,576]{1,2,0:T(8,128)(2,1)S(1)} fusion(bf16[8,128,2048]{1,2,0:T(8,128)(2,1)} %copy-done.5, bf16[2048,576]{0,1:T(8,128)(2,1)} %all-gather.2.cloned.1.call-done), kind=kOutput, calls=%fused_computation.15 | convolution fusion | flops 2417098752 | bytes 7733248 | tf_op jit(solution)/shard_map/htp,pd->thd/dot_general | solution.py:61
  84.1 1.4 copy.42
  85.5 58.2 %reduce-scatter.2.cloned.1.call-done = f32[128,576]{0,1:T(8,128)} async-done(((f32[2048,576]{0,1:T(8,128)}), f32[128,576]{0,1:T(8,128)}) %reduce-scatter.2.cloned.1.call-update) | async-done | bytes 294928 | tf_op jit(solution)/shard_map/reduce_scatter | solution.py:72
  143.7 45.9 %all-reduce.2 = bf16[128,576]{0,1:T(8,128)(2,1)} all-reduce(f32[128,576]{0,1:T(8,128)} %reduce-scatter.2.cloned.1.call-done), channel_id=1, replica_groups=mesh['ctx'=16,'head'=8] {'head'}, use_global_device_ids=true, to_apply=%region_6.7 | all-reduce | flops 73728 | bytes 442368 | tf_op jit(solution)/shard_map/psum | solution.py:73
  (9 shorter events, 0.1 us)
Async XLA Ops:
  7.2 3.7 %copy-start = (bf16[128,4608]{1,0:T(8,128)(2,1)S(1)}, bf16[128,4608]{1,0:T(8,128)(2,1)}, u32[]{:S(2)}) copy-start(bf16[128,4608]{1,0:T(8,128)(2,1)} %param.4) | copy-start | bytes 3538948
  7.2 4.5 %copy-start.3 = (s32[16]{0:T(128)S(1)}, s32[16]{0:T(128)}, u32[]{:S(2)}) copy-start(s32[16]{0:T(128)} %param.6) | copy-start | bytes 196
  7.2 43.3 %all-gather.2.cloned.1.call-start = ((), (), s32[]{:S(2)}) async-start(), calls=%async_computation.1 | async-start | bytes 2506752 | tf_op jit(solution)/shard_map/all_gather | solution.py:47
  7.9 135.8 %reduce-scatter.2.cloned.1.call-start = ((), (), s32[]{:S(2)}) async-start(), calls=%async_computation.2 | async-start | bytes 5013504 | tf_op jit(solution)/shard_map/reduce_scatter | solution.py:72
  58.1 2.7 %copy-start.1 = (bf16[128,8,512]{2,0,1:T(8,128)(2,1)S(1)}, bf16[128,8,512]{2,0,1:T(8,128)(2,1)}, u32[]{:S(2)}) copy-start(bf16[128,8,512]{2,0,1:T(8,128)(2,1)} %copy.37) | copy-start | bytes 3145732
  58.2 2.7 %copy-start.4 = (bf16[2048,576]{0,1:T(8,128)(2,1)S(1)}, bf16[2048,576]{0,1:T(8,128)(2,1)}, u32[]{:S(2)}) copy-start(bf16[2048,576]{0,1:T(8,128)(2,1)} %all-gather.2.cloned.1.call-done) | copy-start | bytes 7077892
  69.0 2.0 %copy-start.5 = (bf16[8,128,2048]{1,2,0:T(8,128)(2,1)}, bf16[8,128,2048]{1,2,0:T(8,128)(2,1)S(1)}, u32[]{:S(2)}) copy-start(bf16[8,128,2048]{1,2,0:T(8,128)(2,1)S(1)} %fusion.1) | copy-start | bytes 12582916
  75.4 1.2 copy-start.2
Sparse Core Ops, SparseCore 0:
  9.6 40.7 all-gather.1
  75.5 68.1 reduce-scatter.1
where the time goes:
time: 197 us; the launch traced here: 196 us
  waiting for transfers between devices  97.2 us (49%)
  blocking collectives  45.9 us (23%)
  matrix products  26.2 us (13%)
  between operations  14.2 us (7%)
  local copies, waits for them, and re-layouts  10.3 us (5%)
  other arithmetic  2.6 us (1%)
    reduce_scatter x1, waiting for transfers between devices, local(): lax.psum_scatter(key_accum, 'ctx', scatter_dimension=0, tiled=True)  58.2 us
    psum x1, blocking collectives, local(): latent_grad = lax.psum(partial_rows, 'head').astype(jnp.bfloat16)  45.9 us
    all_gather x1, waiting for transfers between devices, local(): piece = lax.all_gather(latent_keys, 'ctx', axis=0, tiled=True)  38.2 us
    unnamed x16, local copies, waits for them, and re-layouts  8.29 us
    dot_general x1, matrix products, piece_scores(): jnp.einsum('thd,pd->htp', query_three, piece, preferred_element_type=jnp....  5.59 us
    dot_general x1, matrix products, local(): jnp.einsum('htp,pd->thd', dscore, piece, preferred_element_type=jnp.float32)  5.5 us
    dot_general x1, matrix products, local(): jnp.einsum('the,pe->htp', grad_three, piece[:, :LATENT], preferred_elemen...  4.47 us
    dot_general x1, matrix products, local(): jnp.einsum('htp,thd->pd', dscore, query_three, preferred_element_type=jnp...  4.31 us
  transfers between devices with their start and end apart: 2, of which 2 were waited for; matrix products, arithmetic and copies ran while one was open for 7% of the time, Pallas kernels for 0%

commit v1 on v0

--- a/solution.py
+++ b/solution.py
@@ -7,6 +7,11 @@
 ROPE = 64
 score_scale = 192.0 ** (-0.5)
 masked_value = -1e30
+
+
+def summed_here(value, mesh_axis):
+    terms = lax.all_gather(value, mesh_axis)
+    return jnp.sum(terms, axis=0)
 
 
 def row_positions(block_order, first_row, count, shard_rows):
@@ -70,7 +75,7 @@
         (score_scale * query_accum).astype(jnp.bfloat16).reshape(shard_rows, head_count * kdim)
     )
     partial_rows = lax.psum_scatter(key_accum, "ctx", scatter_dimension=0, tiled=True)
-    latent_grad = lax.psum(partial_rows, "head").astype(jnp.bfloat16)
+    latent_grad = summed_here(partial_rows, "head").astype(jnp.bfloat16)
     return (attended.reshape(shard_rows, head_count * LATENT), query_grad, latent_grad)
 
 

time: 197 us -> 215 us (1.091)
  waiting for transfers between devices: 97.2 us -> 159 us
  blocking collectives: 45.9 us -> 0 us
    all_gather x0 -> x1, waiting for transfers between devices: none -> 51.7 us  [summed_here(): terms = lax.all_gather(value, mesh_axis)]
    psum x1 -> x0, blocking collectives: 45.9 us -> none  [local(): latent_grad = lax.psum(partial_rows, 'head').astype(jnp.bfloat16)]
    reduce_scatter x1, waiting for transfers between devices: 58.2 us -> 68.3 us  [local(): lax.psum_scatter(key_accum, 'ctx', scatter_dimension=0, tiled=True)]
    unnamed x16 -> x17, local copies, waits for them, and re-layouts: 8.29 us -> 9.29 us
  transfers between devices with their start and end apart: 2 -> 3, of which waited for: 2 -> 3; matrix products, arithmetic and copies ran while one was open for 7% -> 6% of each run, Pallas kernels for 0% -> 0%
where the time goes in v1:
time: 215 us; the launch traced here: 214 us
  waiting for transfers between devices  159 us (74%)
  matrix products  26.2 us (12%)
  between operations  13.9 us (6%)
  local copies, waits for them, and re-layouts  11.3 us (5%)
  other arithmetic  3.9 us (2%)
    reduce_scatter x1, waiting for transfers between devices, local(): lax.psum_scatter(key_accum, 'ctx', scatter_dimension=0, tiled=True)  68.3 us
    all_gather x1, waiting for transfers between devices, summed_here(): terms = lax.all_gather(value, mesh_axis)  51.7 us
    all_gather x1, waiting for transfers between devices, local(): piece = lax.all_gather(latent_keys, 'ctx', axis=0, tiled=True)  38.2 us
    unnamed x17, local copies, waits for them, and re-layouts  9.29 us
    dot_general x1, matrix products, piece_scores(): jnp.einsum('thd,pd->htp', query_three, piece, preferred_element_type=jnp....  5.59 us
    dot_general x1, matrix products, local(): jnp.einsum('htp,pd->thd', dscore, piece, preferred_element_type=jnp.float32)  5.5 us
    dot_general x1, matrix products, local(): jnp.einsum('the,pe->htp', grad_three, piece[:, :LATENT], preferred_elemen...  4.47 us
    dot_general x1, matrix products, local(): jnp.einsum('htp,thd->pd', dscore, query_three, preferred_element_type=jnp...  4.31 us
  transfers between devices with their start and end apart: 3, of which 3 were waited for; matrix products, arithmetic and copies ran while one was open for 6% of the time, Pallas kernels for 0%

profile of v1, /device:TPU:0, one launch (start us, length us, event | category | flops | bytes accessed | tf_op | source)
XLA Modules:
  0.0 214.4 jit_solution(8906080239367731311)
XLA Ops:
  7.2 0.0 copy-start
  7.2 0.0 all-gather.4.cloned.1.call-start
  7.2 0.7 all-gather.4.cloned.1.call-update
  7.9 0.0 reduce-scatter.2.cloned.1.call-start
  8.0 1.6 copy.34
  9.6 1.3 copy.37
  10.9 0.0 copy-done
  10.9 0.7 copy.30
  11.7 0.1 select_reduce_fusion.2
  11.8 0.1 select_reduce_fusion.1
  11.9 0.3 broadcast_compare_fusion
  12.2 38.2 %all-gather.4.cloned.1.call-done = bf16[2048,576]{0,1:T(8,128)(2,1)} async-done(((bf16[128,576]{0,1:T(8,128)(2,1)}), bf16[2048,576]{0,1:T(8,128)(2,1)}) %all-gather.4.cloned.1.call-update) | async-done | bytes 2359312 | tf_op jit(solution)/shard_map/all_gather | solution.py:52
  50.5 5.6 %fusion.3 = (f32[8,128]{1,0:T(8,128)S(1)}, f32[2048,128,8]{1,0,2:T(8,128)S(1)}) fusion(pred[128,2048]{0,1:T(8,128)(4,1)S(1)} %broadcast_compare_fusion, bf16[128,8,576]{0,2,1:T(8,128)(2,1)S(1)} %bitcast.71, bf16[2048,576]{0,1:T(8,128)(2,1)} %all-gather.4.cloned.1.call-done), kind=kOutput, calls=%fused_computation.7 | convolution fusion | flops 2422209536 | bytes 12193792 | tf_op jit(solution)/shard_map/thd,pd->htp/dot_general | solution.py:37
  56.1 2.0 select_reduce_fusion
  58.1 0.0 copy-start.1
  58.2 0.0 copy-start.4
  58.2 2.7 %convolution_bitcast_fusion = f32[2048,512]{0,1:T(8,128)S(1)} fusion(bf16[128,8,512]{0,2,1:T(8,128)(2,1)S(1)} %bitcast.67, f32[2048,128,8]{1,0,2:T(8,128)S(1)} %get-tuple-element.13, f32[8,128]{1,0:T(8,128)S(1)} %log_add_fusion, pred[128,2048]{0,1:T(8,128)(4,1)S(1)} %broadcast_compare_fusion), kind=kOutput, calls=%fused_computation.10 | convolution fusion | flops 2157969408 | bytes 13897728 | tf_op jit(solution)/shard_map/htp,the->pe/dot_general | solution.py:70
  60.9 3.7 %multiply_reduce_fusion = (f32[128,8]{0,1:T(8,128)S(1)}, bf16[128,8,512]{2,0,1:T(8,128)(2,1)}) fusion(bf16[128,8,512]{2,0,1:T(8,128)(2,1)S(1)} %copy-done.1, bf16[2048,576]{0,1:T(8,128)(2,1)S(1)} %copy-done.4, f32[2048,128,8]{1,0,2:T(8,128)S(1)} %get-tuple-element.13, f32[8,128]{1,0:T(8,128)S(1)} %log_add_fusion, ...), kind=kOutput, calls=%fused_computation.18 | convolution fusion | flops 2160589824 | bytes 12853248 | tf_op jit(solution)/shard_map/htp,pe->the/dot_general | solution.py:55
  64.6 4.5 %fusion.1 = bf16[8,128,2048]{1,2,0:T(8,128)(2,1)S(1)} fusion(f32[2048,128,8]{1,0,2:T(8,128)S(1)} %get-tuple-element.13, bf16[128,8,512]{0,2,1:T(8,128)(2,1)S(1)} %bitcast.68, f32[8,128]{1,0:T(8,128)S(1)} %bitcast.74, f32[8,128]{1,0:T(8,128)S(1)} %log_add_fusion, pred[128,2048]{0,1:T(8,128)(4,1)S(1)} %broadcast_compare_fusion, bf16[2048,576]{0,1:T(8,128)(2,1)S(1)} %copy-done.4), kind=kOutput, calls=%fused_computation.2 | convolution fusion | flops 2162163712 | bytes 15998976 | tf_op jit(solution)/shard_map/the,pe->htp/dot_general | solution.py:62
  69.0 2.0 copy-done.5
  71.0 4.3 %fusion.4 = f32[2048,576]{0,1:T(8,128)} fusion(f32[2048,512]{0,1:T(8,128)S(1)} %convolution_bitcast_fusion, bf16[8,128,2048]{1,2,0:T(8,128)(2,1)S(1)} %fusion.1, bf16[128,8,576]{0,2,1:T(8,128)(2,1)S(1)} %bitcast.72), kind=kOutput, calls=%fused_computation.9 | convolution fusion | flops 2418278400 | bytes 14286848 | tf_op jit(solution)/shard_map/htp,thd->pd/dot_general | solution.py:67
  75.4 0.0 reduce-scatter.2.cloned.1.call-update
  75.4 0.0 all-gather.6.cloned.1.call-start
  75.4 68.3 %reduce-scatter.2.cloned.1.call-done = f32[128,576]{0,1:T(8,128)} async-done(((f32[2048,576]{0,1:T(8,128)}), f32[128,576]{0,1:T(8,128)}) %reduce-scatter.2.cloned.1.call-update) | async-done | bytes 294928 | tf_op jit(solution)/shard_map/reduce_scatter | solution.py:77
  143.7 0.0 all-gather.6.cloned.1.call-update
  143.8 0.7 copy.33
  144.4 1.3 copy.41
  145.7 5.5 %multiply_convert_fusion = bf16[8,128,576]{1,2,0:T(8,128)(2,1)S(1)} fusion(bf16[8,128,2048]{1,2,0:T(8,128)(2,1)} %copy-done.5, bf16[2048,576]{0,1:T(8,128)(2,1)} %all-gather.4.cloned.1.call-done), kind=kOutput, calls=%fused_computation.16 | convolution fusion | flops 2417098752 | bytes 7733248 | tf_op jit(solution)/shard_map/htp,pd->thd/dot_general | solution.py:66
  151.2 1.4 copy.42
  152.7 51.7 %all-gather.6.cloned.1.call-done = f32[1024,576]{0,1:T(8,128)} async-done(((f32[128,576]{0,1:T(8,128)}), f32[1024,576]{0,1:T(8,128)}) %all-gather.6.cloned.1.call-update) | async-done | bytes 2359312 | tf_op jit(solution)/shard_map/all_gather | solution.py:13
  204.4 2.2 %copy.52 = f32[72,8,8,128]{3,2,1,0:T(8,128)S(1)} copy(f32[72,8,8,128]{3,1,2,0:T(8,128)} %bitcast.70) | data formatting | bytes 4718592
  206.6 1.3 bitcast_reduce_fusion
  (13 shorter events, 0.1 us)
Async XLA Ops:
  7.2 3.7 %copy-start = (bf16[128,4608]{1,0:T(8,128)(2,1)S(1)}, bf16[128,4608]{1,0:T(8,128)(2,1)}, u32[]{:S(2)}) copy-start(bf16[128,4608]{1,0:T(8,128)(2,1)} %param.4) | copy-start | bytes 3538948
  7.2 4.5 %copy-start.3 = (s32[16]{0:T(128)S(1)}, s32[16]{0:T(128)}, u32[]{:S(2)}) copy-start(s32[16]{0:T(128)} %param.6) | copy-start | bytes 196
  7.2 43.3 %all-gather.4.cloned.1.call-start = ((), (), s32[]{:S(2)}) async-start(), calls=%async_computation.1 | async-start | bytes 2506752 | tf_op jit(solution)/shard_map/all_gather | solution.py:52
  7.9 135.8 %reduce-scatter.2.cloned.1.call-start = ((), (), s32[]{:S(2)}) async-start(), calls=%async_computation.2 | async-start | bytes 5013504 | tf_op jit(solution)/shard_map/reduce_scatter | solution.py:77
  58.1 2.7 %copy-start.1 = (bf16[128,8,512]{2,0,1:T(8,128)(2,1)S(1)}, bf16[128,8,512]{2,0,1:T(8,128)(2,1)}, u32[]{:S(2)}) copy-start(bf16[128,8,512]{2,0,1:T(8,128)(2,1)} %copy.37) | copy-start | bytes 3145732
  58.2 2.7 %copy-start.4 = (bf16[2048,576]{0,1:T(8,128)(2,1)S(1)}, bf16[2048,576]{0,1:T(8,128)(2,1)}, u32[]{:S(2)}) copy-start(bf16[2048,576]{0,1:T(8,128)(2,1)} %all-gather.4.cloned.1.call-done) | copy-start | bytes 7077892
  69.0 2.0 copy-start.5
  75.4 68.4 %copy-start.2 = (bf16[128,8,512]{2,0,1:T(8,128)(2,1)S(1)}, bf16[128,8,512]{2,0,1:T(8,128)(2,1)}, u32[]{:S(2)}) copy-start(bf16[128,8,512]{2,0,1:T(8,128)(2,1)} %get-tuple-element.15) | copy-start | bytes 3145732
  75.4 129.0 %all-gather.6.cloned.1.call-start = ((), (), s32[]{:S(2)}) async-start(), calls=%async_computation.3 | async-start | bytes 2654208 | tf_op jit(solution)/shard_map/all_gather | solution.py:13
Sparse Core Ops, SparseCore 0:
  9.6 40.7 all-gather.3
  75.5 68.1 reduce-scatter.1
  145.9 58.4 all-gather.5
